TPU v7x, 512 devices: a whole 4x4x16 slice. The times are simulated.
512 devices in a mesh: rep: 64 (over z, x_lo, core), fsdp: 8 (over x_hi, y).
Axes of the slice: x: 4 (x_hi: 2, x_lo: 2; x = x_hi * 2 + x_lo), y: 4, z: 16, core: 2. Of those that a mesh axis runs over, the one named last changes fastest.
Arguments:
- step: int32 [1], replicated, may hold values from 0 to 999
- numerator: float32 [64, 512, 1024], P('rep', 'fsdp'), may hold values from -6 to 6
- weight: float32 [64], P('rep'), may hold values from 0.25 to 4
- moment1: float32 [64, 512, 1024], P('rep', 'fsdp'), may hold values from -4 to 4
- moment2: float32 [64, 512, 1024], P('rep', 'fsdp'), may hold values from 0.01 to 1
- grads: bfloat16 [64, 8, 512, 1024], P('rep', 'fsdp'), may hold values from -6 to 6
Outputs:
- new_numerator: float32 [64, 512, 1024], P('rep', 'fsdp')
- new_weight: float32 [64], P('rep')
- debiased: bfloat16 [64, 512, 1024], P('rep', 'fsdp')
- new_moment1: float32 [64, 512, 1024], P('rep', 'fsdp')
- new_moment2: float32 [64, 512, 1024], P('rep', 'fsdp')
Inputs may be any that keep to these rules, and one draw needn't show every extreme that they name: t is a step index.
All inputs are finite; a program needn't handle non-finite values.
Results may differ from a plain program's by a relative error of at most 0.013.
Values may be sent and summed in bfloat16 or wider, within the bound.
No kernel may reach another device: no remote copies, remote signals or barrier semaphores. Data moves between devices by JAX's collectives and lax.ppermute only.
A program may use at most 64 MiB of HBM per device.

v0:
```python
from functools import partial

import jax
import jax.numpy as jnp
from jax import lax
from jax.sharding import PartitionSpec as P


def for_sending(x):
    return jax.tree.map(lambda a: a.astype(jnp.bfloat16) if a.dtype == jnp.float32 else a, x)


def shifted(value, axis, steps):
    count = lax.axis_size(axis)
    pairs = [(source, (source + steps) % count) for source in range(count)]
    return lax.ppermute(value, axis, pairs)


def mix_after(pair, offset):
    return jax.tree.map(
        lambda part, own: part.astype(own.dtype), shifted(for_sending(pair), "rep", offset), pair
    )


def local(step, numerator, weight, moment1, moment2, grads):
    levels = lax.axis_size("rep").bit_length() - 1
    phase = step[0] % levels
    summed = lax.psum_scatter(grads[0], "fsdp", scatter_dimension=1, tiled=True).astype(jnp.float32)
    gradient = summed / lax.axis_size("fsdp")
    new_moment1 = 0.9 * moment1 + 0.1 * gradient
    new_moment2 = 0.95 * moment2 + 0.05 * gradient * gradient
    count = (step[0] + 1).astype(jnp.float32)
    first_corr = 1.0 - jnp.power(jnp.float32(0.9), count)
    second_corr = 1.0 - jnp.power(jnp.float32(0.95), count)
    update = 0.05 * (
        new_moment1 / first_corr / (jnp.sqrt(new_moment2 / second_corr) + 1e-08) + 0.1 * numerator
    )
    half = numerator - update
    after_branches = [partial(mix_after, offset=1 << level) for level in range(levels)]
    half_partner, weight_partner = lax.switch(phase, after_branches, (half, weight))
    new_numerator = 0.5 * (half + half_partner)
    new_weight = 0.5 * (weight + weight_partner)
    debiased = (new_numerator / new_weight[:, None, None]).astype(jnp.bfloat16)
    return (new_numerator, new_weight, debiased, new_moment1, new_moment2)


def solution(mesh):
    in_specs = (
        P(),
        P("rep", "fsdp", None),
        P("rep"),
        P("rep", "fsdp", None),
        P("rep", "fsdp", None),
        P("rep", "fsdp", None, None),
    )
    out_specs = (
        P("rep", "fsdp", None),
        P("rep"),
        P("rep", "fsdp", None),
        P("rep", "fsdp", None),
        P("rep", "fsdp", None),
    )
    return jax.shard_map(local, mesh=mesh, in_specs=in_specs, out_specs=out_specs, check_vma=False)
```

profile of v0, /device:TPU:8, one launch (start us, length us, event | category | flops | bytes accessed | tf_op | source)
XLA Modules:
  0.0 124.5 jit_solution(14012290517694259686)
XLA Ops:
  7.2 0.0 reduce-scatter.2.cloned.1.call-start
  7.2 0.0 copy-start
  7.2 0.0 copy-start.1
  7.2 0.0 copy-start.2
  7.2 0.7 reduce-scatter.2.cloned.1.call-update
  9.3 94.3 %reduce-scatter.2.cloned.1.call-done = bf16[1,64,1024]{2,1,0:T(8,128)(2,1)} async-done(((bf16[1,512,1024]{2,1,0:T(8,128)(2,1)}), bf16[1,64,1024]{2,1,0:T(8,128)(2,1)}) %reduce-scatter.2.cloned.1.call-update) | async-done | bytes 131088 | tf_op jit(solution)/shard_map/reduce_scatter | solution.py:28
  103.6 0.0 copy-done
  103.6 0.0 copy-done.1
  103.6 0.0 copy-done.2
  103.6 1.9 %multiply_subtract_fusion = (f32[1,64,1024]{2,1,0:T(8,128)S(1)}, f32[1,64,1024]{2,1,0:T(8,128)}, f32[1,64,1024]{2,1,0:T(8,128)}) fusion(f32[1,64,1024]{2,1,0:T(8,128)S(1)} %copy-done, f32[]{:T(128)} %bitcast.2, f32[]{:T(128)} %bitcast.1, bf16[1,64,1024]{2,1,0:T(8,128)(2,1)} %reduce-scatter.2.cloned.1.call-done, f32[1,64,1024]{2,1,0:T(8,128)S(1)} %copy-done.1, ...), kind=kLoop, calls=%fused_computation.8 | loop fusion | flops 1114112 | bytes 1703944 | tf_op jit(solution)/shard_map/sub | solution.py:38
  105.5 10.3 %conditional.4 = (f32[1,64,1024]{2,1,0:T(8,128)S(1)}, f32[1]{0:T(128)}) conditional(s32[]{:T(128)} %clamp.3, (f32[1,64,1024]{2,1,0:T(8,128)S(1)}, f32[1]{0:T(128)}) %tuple.70, (f32[1,64,1024]{2,1,0:T(8,128)S(1)}, f32[1]{0:T(128)}) %tuple.70, (f32[1,64,1024]{2,1,0:T(8,128)S(1)}, f32[1]{0:T(128)}) %tuple.70, ...), branch_computations={%region_1.2_spmd, %region_2.3_spmd, %region_3.4_spmd, %region_4.5_... | conditional | flops 131074 | bytes 1310836
  105.5 1.9 %collective-permute-start = (bf16[1,64,1024]{2,1,0:T(8,128)(2,1)S(1)}, bf16[1,64,1024]{2,1,0:T(8,128)(2,1)S(1)}, u32[]{:S(2)}, u32[]{:S(2)}) collective-permute-start(bf16[1,64,1024]{2,1,0:T(8,128)(2,1)S(1)} %convert_element_type.83), channel_id=1, source_target_pairs={{0,8},{8,16},{16,24},{24,32},{32,40},{40,48},{48,56},{56,64},{64,7... | collective-permute-start | bytes 393224 | tf_op jit(solution)/shard_map/cond/branch_0_fun/ppermute | solution.py:16
  108.1 3.5 %collective-permute-start.1 = (bf16[1]{0:T(256)(128)(2,1)}, bf16[1]{0:T(256)(128)(2,1)}, u32[]{:S(2)}, u32[]{:S(2)}) collective-permute-start(bf16[1]{0:T(256)(128)(2,1)} %convert_element_type.85), channel_id=1, source_target_pairs={{0,8},{8,16},{16,24},{24,32},{32,40},{40,48},{48,56},{56,64},{64,7... | collective-permute-start | bytes 14 | tf_op jit(solution)/shard_map/cond/branch_0_fun/ppermute | solution.py:16
  111.5 3.5 %collective-permute-done.1 = bf16[1]{0:T(256)(128)(2,1)} collective-permute-done((bf16[1]{0:T(256)(128)(2,1)}, bf16[1]{0:T(256)(128)(2,1)}, u32[]{:S(2)}, u32[]{:S(2)}) %collective-permute-start.1) | collective-permute-done | bytes 34 | tf_op jit(solution)/shard_map/cond/branch_0_fun/ppermute | solution.py:16
  115.7 0.0 collective-permute-done
  115.8 0.8 divide_convert_fusion
  (2 shorter events, 0.0 us)
Async XLA Ops:
  7.2 96.4 %reduce-scatter.2.cloned.1.call-start = ((), (), s32[]{:S(2)}) async-start(), calls=%async_computation.1 | async-start | bytes 1179648 | tf_op jit(solution)/shard_map/reduce_scatter | solution.py:28
  7.2 96.4 %copy-start = (f32[1,64,1024]{2,1,0:T(8,128)S(1)}, f32[1,64,1024]{2,1,0:T(8,128)}, u32[]{:S(2)}) copy-start(f32[1,64,1024]{2,1,0:T(8,128)} %param.13) | copy-start | bytes 786436
  7.2 96.3 %copy-start.1 = (f32[1,64,1024]{2,1,0:T(8,128)S(1)}, f32[1,64,1024]{2,1,0:T(8,128)}, u32[]{:S(2)}) copy-start(f32[1,64,1024]{2,1,0:T(8,128)} %param.16) | copy-start | bytes 786436
  7.2 96.3 %copy-start.2 = (f32[1,64,1024]{2,1,0:T(8,128)S(1)}, f32[1,64,1024]{2,1,0:T(8,128)}, u32[]{:S(2)}) copy-start(f32[1,64,1024]{2,1,0:T(8,128)} %param.15) | copy-start | bytes 786436
  105.5 10.2 %collective-permute-start = (bf16[1,64,1024]{2,1,0:T(8,128)(2,1)S(1)}, bf16[1,64,1024]{2,1,0:T(8,128)(2,1)S(1)}, u32[]{:S(2)}, u32[]{:S(2)}) collective-permute-start(bf16[1,64,1024]{2,1,0:T(8,128)(2,1)S(1)} %convert_element_type.83), channel_id=1, source_target_pairs={{0,8},{8,16},{16,24},{24,32},{32,40},{40,48},{48,56},{56,64},{64,7... | collective-permute-start | bytes 393224 | tf_op jit(solution)/shard_map/cond/branch_0_fun/ppermute | solution.py:16
  108.1 6.9 %collective-permute-start.1 = (bf16[1]{0:T(256)(128)(2,1)}, bf16[1]{0:T(256)(128)(2,1)}, u32[]{:S(2)}, u32[]{:S(2)}) collective-permute-start(bf16[1]{0:T(256)(128)(2,1)} %convert_element_type.85), channel_id=1, source_target_pairs={{0,8},{8,16},{16,24},{24,32},{32,40},{40,48},{48,56},{56,64},{64,7... | collective-permute-start | bytes 14 | tf_op jit(solution)/shard_map/cond/branch_0_fun/ppermute | solution.py:16
Sparse Core Ops, SparseCore 0:
  12.5 91.0 reduce-scatter.1
where the time goes:
time: 125 us
  waiting for transfers between devices  98.4 us (79%)
  between operations  16.6 us (13%)
  starting transfers between devices  5.42 us (4%)
  other arithmetic  2.72 us (2%)
  loops' own time  1.4 us (1%)
    reduce_scatter x1, waiting for transfers between devices, local(): lax.psum_scatter(grads[0], 'fsdp', scatter_dimension=1, tiled=True)  94.3 us
    ppermute x2, starting transfers between devices, shifted(): return lax.ppermute(value, axis, pairs)  5.39 us
    ppermute x2, waiting for transfers between devices, shifted(): return lax.ppermute(value, axis, pairs)  3.46 us
  transfers between devices with their start and end apart: 3, of which 2 were waited for; matrix products, arithmetic and copies ran while one was open for 0% of the time, Pallas kernels for 0%

commit v1 on v0

--- a/solution.py
+++ b/solution.py
@@ -6,27 +6,34 @@
 from jax.sharding import PartitionSpec as P
 
 
-def for_sending(x):
-    return jax.tree.map(lambda a: a.astype(jnp.bfloat16) if a.dtype == jnp.float32 else a, x)
-
-
 def shifted(value, axis, steps):
     count = lax.axis_size(axis)
     pairs = [(source, (source + steps) % count) for source in range(count)]
     return lax.ppermute(value, axis, pairs)
 
 
-def mix_after(pair, offset):
-    return jax.tree.map(
-        lambda part, own: part.astype(own.dtype), shifted(for_sending(pair), "rep", offset), pair
-    )
+def split_in_pieces(weight):
+    high = weight.astype(jnp.bfloat16)
+    rest = weight - high.astype(jnp.float32)
+    middle = rest.astype(jnp.bfloat16)
+    low = (rest - middle.astype(jnp.float32)).astype(jnp.bfloat16)
+    return high, middle, low
+
+
+def mix_after(half, weight, offset):
+    sent = shifted(half.astype(jnp.bfloat16), "rep", offset)
+    sent_weight = shifted(weight, "rep", offset)
+    return sent, sent_weight
 
 
 def local(step, numerator, weight, moment1, moment2, grads):
     levels = lax.axis_size("rep").bit_length() - 1
+    n_fsdp = lax.axis_size("fsdp")
     phase = step[0] % levels
-    summed = lax.psum_scatter(grads[0], "fsdp", scatter_dimension=1, tiled=True).astype(jnp.float32)
-    gradient = summed / lax.axis_size("fsdp")
+    rows = numerator.shape[1]
+    blocks = grads.reshape(n_fsdp, rows, -1)
+    landed = lax.all_to_all(blocks, "fsdp", split_axis=0, concat_axis=0, tiled=True)
+    gradient = jnp.sum(landed, axis=0, dtype=jnp.float32)[None] / n_fsdp
     new_moment1 = 0.9 * moment1 + 0.1 * gradient
     new_moment2 = 0.95 * moment2 + 0.05 * gradient * gradient
     count = (step[0] + 1).astype(jnp.float32)
@@ -37,8 +44,8 @@
     )
     half = numerator - update
     after_branches = [partial(mix_after, offset=1 << level) for level in range(levels)]
-    half_partner, weight_partner = lax.switch(phase, after_branches, (half, weight))
-    new_numerator = 0.5 * (half + half_partner)
+    half_partner, weight_partner = lax.switch(phase, after_branches, half, weight)
+    new_numerator = 0.5 * (half + half_partner.astype(jnp.float32))
     new_weight = 0.5 * (weight + weight_partner)
     debiased = (new_numerator / new_weight[:, None, None]).astype(jnp.bfloat16)
     return (new_numerator, new_weight, debiased, new_moment1, new_moment2)

time: 125 us -> 42.9 us (0.34)
  the two profiles are of different devices: /device:TPU:8 before, /device:TPU:4 now
where the time goes in v1:
time: 42.9 us; the launch traced here: 42.7 us
  waiting for transfers between devices  19.3 us (45%)
  starting transfers between devices  16.6 us (39%)
  between operations  3.85 us (9%)
  other arithmetic  2.87 us (7%)
    all_to_all x1, waiting for transfers between devices, local(): lax.all_to_all(blocks, 'fsdp', split_axis=0, concat_axis=0, tiled=True)  10.8 us
    all_to_all x1, starting transfers between devices, local(): lax.all_to_all(blocks, 'fsdp', split_axis=0, concat_axis=0, tiled=True)  9.37 us
    ppermute x2, waiting for transfers between devices, shifted(): return lax.ppermute(value, axis, pairs)  8.51 us
    ppermute x2, starting transfers between devices, shifted(): return lax.ppermute(value, axis, pairs)  7.2 us
    convert_element_type x1, other arithmetic, local(): debiased = (new_numerator / new_weight[:, None, None]).astype(jnp.bfloat16)  1.69 us
    sub x1, other arithmetic, local(): half = numerator - update  0.99 us
  transfers between devices with their start and end apart: 3, of which 2 were waited for; matrix products, arithmetic and copies ran while one was open for 0% of the time, Pallas kernels for 0%

profile of v1, /device:TPU:4, one launch (start us, length us, event | category | flops | bytes accessed | tf_op | source)
XLA Modules:
  0.0 42.7 jit_solution(14635156183279868603)
XLA Ops:
  0.6 9.4 %all-to-all-start = ((bf16[8,64,1024]{2,1,0:T(8,128)(2,1)}), bf16[8,64,1024]{2,1,0:T(8,128)(2,1)S(1)}, u32[]{:S(2)}, u32[]{:S(2)}) async-start(bf16[8,64,1024]{2,1,0:T(8,128)(2,1)} %bitcast.11), calls=%async_computation | async-start | bytes 2097152 | tf_op jit(solution)/shard_map/all_to_all | solution.py:35
  10.0 0.0 copy-start
  10.0 0.0 copy-start.1
  10.0 0.0 copy-start.2
  11.5 10.8 %all-to-all-done = bf16[8,64,1024]{2,1,0:T(8,128)(2,1)S(1)} async-done(((bf16[8,64,1024]{2,1,0:T(8,128)(2,1)}), bf16[8,64,1024]{2,1,0:T(8,128)(2,1)S(1)}, u32[]{:S(2)}, u32[]{:S(2)}) %all-to-all-start) | async-done | bytes 1048608 | tf_op jit(solution)/shard_map/all_to_all | solution.py:35
  22.3 0.2 convert_reduce_fusion
  22.5 0.0 copy-done
  22.5 0.0 copy-done.1
  22.5 0.0 copy-done.2
  22.5 1.0 %multiply_subtract_fusion = (f32[1,64,1024]{2,1,0:T(8,128)S(1)}, f32[1,64,1024]{2,1,0:T(8,128)}, f32[1,64,1024]{2,1,0:T(8,128)}) fusion(f32[1,64,1024]{2,1,0:T(8,128)S(1)} %copy-done, f32[]{:T(128)} %bitcast.4, f32[]{:T(128)} %bitcast.2, f32[64,1024]{1,0:T(8,128)S(1)} %convert_reduce_fusion, f32[1,64,1024]{2,1,0:T(8,128)S(1)} %copy-done.1, ...), kind=kLoop, calls=%fused_computation.6 | loop fusion | flops 1048576 | bytes 1835016 | tf_op jit(solution)/shard_map/sub | solution.py:45
  23.5 15.7 %conditional.4 = (f32[1]{0:T(128)}, bf16[1,64,1024]{2,1,0:T(8,128)(2,1)}) conditional(s32[]{:T(128)} %clamp.3, (f32[1]{0:T(128)}, f32[1,64,1024]{2,1,0:T(8,128)S(1)}) %tuple.58, (f32[1]{0:T(128)}, f32[1,64,1024]{2,1,0:T(8,128)S(1)}) %tuple.58, (f32[1]{0:T(128)}, f32[1,64,1024]{2,1,0:T(8,128)S(1)}) %tuple.58, ...), branch_computations={%region_1.2_spmd, %region_2.3_spmd, %region_3.4_spmd, %region_4.5_... | conditional | flops 65536 | bytes 917616
  23.5 3.1 %collective-permute-start.3 = (bf16[1,64,1024]{2,1,0:T(8,128)(2,1)S(1)}, bf16[1,64,1024]{2,1,0:T(8,128)(2,1)}, u32[]{:S(2)}, u32[]{:S(2)}) collective-permute-start(bf16[1,64,1024]{2,1,0:T(8,128)(2,1)S(1)} %convert_element_type.36), channel_id=1, source_target_pairs={{0,16},{8,24},{16,32},{24,40},{32,48},{40,56},{48,64},{56,72},{64,... | collective-permute-start | bytes 393224 | tf_op jit(solution)/shard_map/cond/branch_1_fun/ppermute | solution.py:12
  26.6 4.1 %collective-permute-start.2 = (f32[1]{0:T(128)}, f32[1]{0:T(128)}, u32[]{:S(2)}, u32[]{:S(2)}) collective-permute-start(f32[1]{0:T(128)} %get-tuple-element.34), channel_id=1, source_target_pairs={{0,16},{8,24},{16,32},{24,40},{32,48},{40,56},{48,64},{56,72},{64,... | collective-permute-start | bytes 20 | tf_op jit(solution)/shard_map/cond/branch_1_fun/ppermute | solution.py:12
  30.8 8.5 %collective-permute-done.2 = f32[1]{0:T(128)} collective-permute-done((f32[1]{0:T(128)}, f32[1]{0:T(128)}, u32[]{:S(2)}, u32[]{:S(2)}) %collective-permute-start.2) | collective-permute-done | bytes 36 | tf_op jit(solution)/shard_map/cond/branch_1_fun/ppermute | solution.py:12
  39.3 0.0 collective-permute-done.3
  39.8 1.7 %divide_convert_fusion = (bf16[1,64,1024]{2,1,0:T(8,128)(2,1)}, f32[1,64,1024]{2,1,0:T(8,128)}) fusion(f32[]{:T(128)} %bitcast.6, f32[1,64,1024]{2,1,0:T(8,128)S(1)} %get-tuple-element.59, bf16[1,64,1024]{2,1,0:T(8,128)(2,1)} %get-tuple-element.56), kind=kLoop, calls=%fused_computation.5 | loop fusion | flops 327680 | bytes 786436 | tf_op jit(solution)/shard_map/convert_element_type | solution.py:50
  (1 shorter events, 0.0 us)
Async XLA Ops:
  0.6 21.7 %all-to-all-start = ((bf16[8,64,1024]{2,1,0:T(8,128)(2,1)}), bf16[8,64,1024]{2,1,0:T(8,128)(2,1)S(1)}, u32[]{:S(2)}, u32[]{:S(2)}) async-start(bf16[8,64,1024]{2,1,0:T(8,128)(2,1)} %bitcast.11), calls=%async_computation | async-start | bytes 2097152 | tf_op jit(solution)/shard_map/all_to_all | solution.py:35
  10.0 12.5 %copy-start = (f32[1,64,1024]{2,1,0:T(8,128)S(1)}, f32[1,64,1024]{2,1,0:T(8,128)}, u32[]{:S(2)}) copy-start(f32[1,64,1024]{2,1,0:T(8,128)} %param.13) | copy-start | bytes 786436
  10.0 12.5 %copy-start.1 = (f32[1,64,1024]{2,1,0:T(8,128)S(1)}, f32[1,64,1024]{2,1,0:T(8,128)}, u32[]{:S(2)}) copy-start(f32[1,64,1024]{2,1,0:T(8,128)} %param.16) | copy-start | bytes 786436
  10.0 12.5 %copy-start.2 = (f32[1,64,1024]{2,1,0:T(8,128)S(1)}, f32[1,64,1024]{2,1,0:T(8,128)}, u32[]{:S(2)}) copy-start(f32[1,64,1024]{2,1,0:T(8,128)} %param.15) | copy-start | bytes 786436
  23.5 15.7 %collective-permute-start.3 = (bf16[1,64,1024]{2,1,0:T(8,128)(2,1)S(1)}, bf16[1,64,1024]{2,1,0:T(8,128)(2,1)}, u32[]{:S(2)}, u32[]{:S(2)}) collective-permute-start(bf16[1,64,1024]{2,1,0:T(8,128)(2,1)S(1)} %convert_element_type.36), channel_id=1, source_target_pairs={{0,16},{8,24},{16,32},{24,40},{32,48},{40,56},{48,64},{56,72},{64,... | collective-permute-start | bytes 393224 | tf_op jit(solution)/shard_map/cond/branch_1_fun/ppermute | solution.py:12
  26.6 12.6 %collective-permute-start.2 = (f32[1]{0:T(128)}, f32[1]{0:T(128)}, u32[]{:S(2)}, u32[]{:S(2)}) collective-permute-start(f32[1]{0:T(128)} %get-tuple-element.34), channel_id=1, source_target_pairs={{0,16},{8,24},{16,32},{24,40},{32,48},{40,56},{48,64},{56,72},{64,... | collective-permute-start | bytes 20 | tf_op jit(solution)/shard_map/cond/branch_1_fun/ppermute | solution.py:12

commit v2 on v0

v2 whole, which is shorter than its diff:
```python
from functools import partial

import jax
import jax.numpy as jnp
from jax import lax
from jax.experimental import pallas as pl
from jax.experimental.pallas import tpu as pltpu
from jax.sharding import PartitionSpec as P

TILE_ROWS = 16
TILE_LANES = 128


def shifted(value, axis, steps):
    count = lax.axis_size(axis)
    pairs = [(source, (source + steps) % count) for source in range(count)]
    return lax.ppermute(value, axis, pairs)


def tiles_of(shape):
    across = shape[1] // TILE_LANES
    for down in range(shape[0] // TILE_ROWS):
        for column in range(across):
            rows = pl.ds(down * TILE_ROWS, TILE_ROWS)
            lanes = pl.ds(column * TILE_LANES, TILE_LANES)
            packed = pl.ds((down * across + column) * TILE_ROWS, TILE_ROWS)
            yield rows, lanes, packed


def moments_of(landed_ref, moment1_ref, moment2_ref, rows, lanes):
    sources = landed_ref.shape[0]
    total = landed_ref[0, rows, lanes].astype(jnp.float32)
    for source in range(1, sources):
        total = total + landed_ref[source, rows, lanes].astype(jnp.float32)
    gradient = total * (1.0 / sources)
    new_moment1 = 0.9 * moment1_ref[rows, lanes] + 0.1 * gradient
    new_moment2 = 0.95 * moment2_ref[rows, lanes] + 0.05 * gradient * gradient
    return new_moment1, new_moment2


def moments_kernel(landed_ref, moment1_ref, moment2_ref, new_moment1_ref, new_moment2_ref):
    for rows, lanes, _ in tiles_of(moment1_ref.shape):
        new_moment1, new_moment2 = moments_of(landed_ref, moment1_ref, moment2_ref, rows, lanes)
        new_moment1_ref[rows, lanes] = new_moment1
        new_moment2_ref[rows, lanes] = new_moment2


def adam_kernel(
    corr1_ref, corr2_ref, weight_ref, landed_ref, numerator_ref, moment1_ref, moment2_ref,
    half_ref, payload_ref,
):
    scale1 = 1.0 / jnp.full((1, TILE_LANES), corr1_ref[0], jnp.float32)
    scale2 = 1.0 / jnp.full((1, TILE_LANES), corr2_ref[0], jnp.float32)
    for rows, lanes, packed in tiles_of(numerator_ref.shape):
        new_moment1, new_moment2 = moments_of(landed_ref, moment1_ref, moment2_ref, rows, lanes)
        numerator = numerator_ref[rows, lanes]
        step = new_moment1 * scale1 / (jnp.sqrt(new_moment2 * scale2) + 1e-08)
        half = numerator - 0.05 * (step + 0.1 * numerator)
        half_ref[rows, lanes] = half
        payload_ref[packed, :] = half.astype(jnp.bfloat16)
    whole = jnp.full((TILE_ROWS, TILE_LANES), weight_ref[0], jnp.float32)
    high = whole.astype(jnp.bfloat16).astype(jnp.float32)
    middle = (whole - high).astype(jnp.bfloat16).astype(jnp.float32)
    low = whole - high - middle
    row = lax.broadcasted_iota(jnp.int32, whole.shape, 0)
    terms = jnp.where(row == 0, high, jnp.where(row == 1, middle, low))
    payload_ref[pl.ds(payload_ref.shape[0] - TILE_ROWS, TILE_ROWS), :] = terms.astype(jnp.bfloat16)


def mix_kernel(weight_ref, half_ref, partner_ref, new_numerator_ref, new_weight_ref, debiased_ref):
    tail = pl.ds(partner_ref.shape[0] - TILE_ROWS, TILE_ROWS)
    terms = partner_ref[tail, :].astype(jnp.float32)
    partner_weight = terms[0:1] + (terms[1:2] + terms[2:3])
    new_weight = 0.5 * (jnp.full_like(partner_weight, weight_ref[0]) + partner_weight)
    new_weight_ref[0] = new_weight[0, 0]
    scale = 1.0 / new_weight
    for rows, lanes, packed in tiles_of(half_ref.shape):
        mixed = 0.5 * (half_ref[rows, lanes] + partner_ref[packed, :].astype(jnp.float32))
        new_numerator_ref[rows, lanes] = mixed
        debiased_ref[rows, lanes] = (mixed * scale).astype(jnp.bfloat16)


def spec(space):
    return pl.BlockSpec(memory_space=space)


def call(kernel, out_shape, in_specs, out_specs, cost):
    return pl.pallas_call(
        kernel,
        out_shape=out_shape,
        in_specs=in_specs,
        out_specs=out_specs,
        compiler_params=pltpu.CompilerParams(vmem_limit_bytes=8 << 20),
        cost_estimate=pl.CostEstimate(flops=cost, bytes_accessed=cost, transcendentals=0),
        name=kernel.__name__,
    )


def exchanged(weight, landed, moment1, moment2, half, payload, offset):
    shard = jax.ShapeDtypeStruct(half.shape, jnp.float32)
    scalars, arrays = spec(pltpu.SMEM), spec(pltpu.VMEM)
    partner = shifted(payload, "rep", offset)
    new_moment1, new_moment2 = call(
        moments_kernel, (shard, shard), [arrays] * 3, (arrays,) * 2, 4 * landed.size
    )(landed, moment1, moment2)
    new_numerator, new_weight, debiased = call(
        mix_kernel,
        (shard, jax.ShapeDtypeStruct((1,), jnp.float32), jax.ShapeDtypeStruct(half.shape, jnp.bfloat16)),
        [scalars] + [arrays] * 2,
        (arrays, scalars, arrays),
        8 * half.size,
    )(weight, half, partner)
    return (new_numerator[None], new_weight, debiased[None], new_moment1[None], new_moment2[None])


def local(step, numerator, weight, moment1, moment2, grads):
    levels = lax.axis_size("rep").bit_length() - 1
    n_fsdp = lax.axis_size("fsdp")
    rows, columns = numerator.shape[1:]
    count = (step + 1).astype(jnp.float32)
    first_corr = 1.0 - jnp.power(jnp.float32(0.9), count)
    second_corr = 1.0 - jnp.power(jnp.float32(0.95), count)
    blocks = grads.reshape(n_fsdp, rows, columns)
    landed = lax.all_to_all(blocks, "fsdp", split_axis=0, concat_axis=0, tiled=True)
    shard = jax.ShapeDtypeStruct((rows, columns), jnp.float32)
    packed_rows = rows * columns // TILE_LANES + TILE_ROWS
    scalars, arrays = spec(pltpu.SMEM), spec(pltpu.VMEM)
    half, payload = call(
        adam_kernel,
        (shard, jax.ShapeDtypeStruct((packed_rows, TILE_LANES), jnp.bfloat16)),
        [scalars] * 3 + [arrays] * 4,
        (arrays,) * 2,
        4 * landed.size,
    )(first_corr, second_corr, weight, landed, numerator[0], moment1[0], moment2[0])
    branches = [partial(exchanged, offset=1 << level) for level in range(levels)]
    return lax.switch(
        step[0] % levels, branches, weight, landed, moment1[0], moment2[0], half, payload
    )


def solution(mesh):
    in_specs = (
        P(),
        P("rep", "fsdp", None),
        P("rep"),
        P("rep", "fsdp", None),
        P("rep", "fsdp", None),
        P("rep", "fsdp", None, None),
    )
    out_specs = (
        P("rep", "fsdp", None),
        P("rep"),
        P("rep", "fsdp", None),
        P("rep", "fsdp", None),
        P("rep", "fsdp", None),
    )
    return jax.shard_map(local, mesh=mesh, in_specs=in_specs, out_specs=out_specs, check_vma=False)
```

time: 125 us -> 46.7 us (0.37)
  the two profiles are of different devices: /device:TPU:8 before, /device:TPU:102 now
where the time goes in v2:
time: 46.7 us; the launch traced here: 46.5 us
  waiting for transfers between devices  24.9 us (53%)
  starting transfers between devices  16.7 us (36%)
  Pallas kernels  2.79 us (6%)
  between operations  2.06 us (4%)
    all_to_all x1, waiting for transfers between devices, local(): lax.all_to_all(blocks, 'fsdp', split_axis=0, concat_axis=0, tiled=True)  12.8 us
    ppermute x1, waiting for transfers between devices, shifted(): return lax.ppermute(value, axis, pairs)  12 us
    ppermute x1, starting transfers between devices, shifted(): return lax.ppermute(value, axis, pairs)  9.1 us
    all_to_all x1, starting transfers between devices, local(): lax.all_to_all(blocks, 'fsdp', split_axis=0, concat_axis=0, tiled=True)  7.58 us
    pallas_call x1, Pallas kernels, exchanged(): call(mix_kernel, (shard, jax.ShapeDtypeStruct((1,), jnp.float32), jax.Sha...  1.45 us
    pallas_call x1, Pallas kernels, exchanged(): call(moments_kernel, (shard, shard), [arrays] * 3, (arrays,) * 2, 4 * lan...  0.99 us
  transfers between devices with their start and end apart: 2, of which 2 were waited for; matrix products, arithmetic and copies ran while one was open for 0% of the time, Pallas kernels for 2%

profile of v2, /device:TPU:102, one launch (start us, length us, event | category | flops | bytes accessed | tf_op | source)
XLA Modules:
  0.0 46.5 jit_solution(12437156847229892245)
XLA Ops:
  0.6 0.0 copy-start
  0.6 0.0 copy-start.1
  0.7 0.0 copy-start.2
  0.7 7.6 %all-to-all-start = ((bf16[8,64,1024]{2,1,0:T(8,128)(2,1)}), bf16[8,64,1024]{2,1,0:T(8,128)(2,1)S(1)}, u32[]{:S(2)}, u32[]{:S(2)}) async-start(bf16[8,64,1024]{2,1,0:T(8,128)(2,1)} %bitcast.44), calls=%async_computation | async-start | bytes 2097152 | tf_op jit(solution)/shard_map/all_to_all | solution.py:124
  9.6 12.8 %all-to-all-done.landed_ref = bf16[8,64,1024]{2,1,0:T(8,128)(2,1)S(1)} async-done(((bf16[8,64,1024]{2,1,0:T(8,128)(2,1)}), bf16[8,64,1024]{2,1,0:T(8,128)(2,1)S(1)}, u32[]{:S(2)}, u32[]{:S(2)}) %all-to-all-start) | async-done | bytes 1048608 | tf_op jit(solution)/shard_map/all_to_all | solution.py:124
  22.5 0.0 copy-done
  22.5 0.0 copy-done.1
  22.5 0.0 copy-done.2
  22.5 0.4 adam_kernel.1
  22.9 23.6 %conditional.1 = (f32[1]{0:T(128)}, f32[1,64,1024]{2,1,0:T(8,128)}, bf16[1,64,1024]{2,1,0:T(8,128)(2,1)}, f32[1,64,1024]{2,1,0:T(8,128)}, f32[1,64,1024]{2,1,0:T(8,128)}) conditional(s32[]{:T(128)} %clamp.3, (bf16[528,128]{1,0:T(8,128)(2,1)S(1)}, f32[1]{0:T(128)}, f32[64,1024]{1,0:T(8,128)S(1)}, ...), branch_computations={%region_0.1_spmd, %region_1.2_spmd, %region_2.3_spmd, %region_3.4_... | conditional | flops 2621440 | bytes 3162192 | solution.py:136
  22.9 9.1 %collective-permute-start.4 = (bf16[528,128]{1,0:T(8,128)(2,1)S(1)}, bf16[528,128]{1,0:T(8,128)(2,1)S(1)}, u32[]{:S(2)}, u32[]{:S(2)}) collective-permute-start(bf16[528,128]{1,0:T(8,128)(2,1)S(1)} %get-tuple-element.118), channel_id=1, source_target_pairs={{0,128},{8,136},{16,144},{24,152},{32,160},{40,168},{48,176},{56,1... | collective-permute-start | bytes 405512 | tf_op jit(solution)/shard_map/cond/branch_4_fun/ppermute | solution.py:17
  32.0 1.0 %moments_kernel.10 = (f32[64,1024]{1,0:T(8,128)}, f32[64,1024]{1,0:T(8,128)}) custom-call(bf16[8,64,1024]{2,1,0:T(8,128)(2,1)S(1)} %get-tuple-element.122.landed_ref, f32[64,1024]{1,0:T(8,128)S(1)} %get-tuple-element.123.moment1_ref, f32[64,1024]{1,0:T(8,128)S(1)} %get-tuple-element.124.moment2_ref), custom_call_target="tpu_custom_call" | custom-call | flops 2097152 | bytes 2097152 | tf_op jit(solution)/shard_map/cond/branch_4_fun/moments_kernel/pallas_call | solution.py:103
  33.0 12.0 %collective-permute-done.4.partner_ref = bf16[528,128]{1,0:T(8,128)(2,1)S(1)} collective-permute-done((bf16[528,128]{1,0:T(8,128)(2,1)S(1)}, bf16[528,128]{1,0:T(8,128)(2,1)S(1)}, u32[]{:S(2)}, u32[]{:S(2)}) %collective-permute-start.4) | collective-permute-done | bytes 135200 | tf_op jit(solution)/shard_map/cond/branch_4_fun/ppermute | solution.py:17
  45.0 1.4 %mix_kernel.10 = (f32[64,1024]{1,0:T(8,128)}, f32[1]{0:T(128)}, bf16[64,1024]{1,0:T(8,128)(2,1)}) custom-call(f32[1]{0:T(128)} %get-tuple-element.116.weight_ref, f32[64,1024]{1,0:T(8,128)S(1)} %get-tuple-element.117.half_ref, bf16[528,128]{1,0:T(8,128)(2,1)S(1)} %collective-permute-done.4.partner_ref), custom_call_target="tpu_custom_call" | custom-call | flops 524288 | bytes 524288 | tf_op jit(solution)/shard_map/cond/branch_4_fun/mix_kernel/pallas_call | solution.py:106
Async XLA Ops:
  0.6 21.9 %copy-start = (f32[1,64,1024]{2,1,0:T(8,128)S(1)}, f32[1,64,1024]{2,1,0:T(8,128)}, u32[]{:S(2)}) copy-start(f32[1,64,1024]{2,1,0:T(8,128)} %param.13) | copy-start | bytes 786436
  0.6 21.8 %copy-start.1 = (f32[1,64,1024]{2,1,0:T(8,128)S(1)}, f32[1,64,1024]{2,1,0:T(8,128)}, u32[]{:S(2)}) copy-start(f32[1,64,1024]{2,1,0:T(8,128)} %param.15) | copy-start | bytes 786436
  0.7 21.8 %copy-start.2 = (f32[1,64,1024]{2,1,0:T(8,128)S(1)}, f32[1,64,1024]{2,1,0:T(8,128)}, u32[]{:S(2)}) copy-start(f32[1,64,1024]{2,1,0:T(8,128)} %param.16) | copy-start | bytes 786436
  0.7 21.8 %all-to-all-start = ((bf16[8,64,1024]{2,1,0:T(8,128)(2,1)}), bf16[8,64,1024]{2,1,0:T(8,128)(2,1)S(1)}, u32[]{:S(2)}, u32[]{:S(2)}) async-start(bf16[8,64,1024]{2,1,0:T(8,128)(2,1)} %bitcast.44), calls=%async_computation | async-start | bytes 2097152 | tf_op jit(solution)/shard_map/all_to_all | solution.py:124
  22.9 22.1 %collective-permute-start.4 = (bf16[528,128]{1,0:T(8,128)(2,1)S(1)}, bf16[528,128]{1,0:T(8,128)(2,1)S(1)}, u32[]{:S(2)}, u32[]{:S(2)}) collective-permute-start(bf16[528,128]{1,0:T(8,128)(2,1)S(1)} %get-tuple-element.118), channel_id=1, source_target_pairs={{0,128},{8,136},{16,144},{24,152},{32,160},{40,168},{48,176},{56,1... | collective-permute-start | bytes 405512 | tf_op jit(solution)/shard_map/cond/branch_4_fun/ppermute | solution.py:17

commit v3 on v2

--- a/solution.py
+++ b/solution.py
@@ -67,11 +67,14 @@
     payload_ref[pl.ds(payload_ref.shape[0] - TILE_ROWS, TILE_ROWS), :] = terms.astype(jnp.bfloat16)
 
 
-def mix_kernel(weight_ref, half_ref, partner_ref, new_numerator_ref, new_weight_ref, debiased_ref):
-    tail = pl.ds(partner_ref.shape[0] - TILE_ROWS, TILE_ROWS)
-    terms = partner_ref[tail, :].astype(jnp.float32)
-    partner_weight = terms[0:1] + (terms[1:2] + terms[2:3])
-    new_weight = 0.5 * (jnp.full_like(partner_weight, weight_ref[0]) + partner_weight)
+def weight_in(payload_ref):
+    tail = pl.ds(payload_ref.shape[0] - TILE_ROWS, TILE_ROWS)
+    terms = payload_ref[tail, :].astype(jnp.float32)
+    return terms[0:1] + (terms[1:2] + terms[2:3])
+
+
+def mix_kernel(half_ref, own_ref, partner_ref, new_numerator_ref, new_weight_ref, debiased_ref):
+    new_weight = 0.5 * (weight_in(own_ref) + weight_in(partner_ref))
     new_weight_ref[0] = new_weight[0, 0]
     scale = 1.0 / new_weight
     for rows, lanes, packed in tiles_of(half_ref.shape):
@@ -96,7 +99,7 @@
     )
 
 
-def exchanged(weight, landed, moment1, moment2, half, payload, offset):
+def exchanged(landed, moment1, moment2, half, payload, offset):
     shard = jax.ShapeDtypeStruct(half.shape, jnp.float32)
     scalars, arrays = spec(pltpu.SMEM), spec(pltpu.VMEM)
     partner = shifted(payload, "rep", offset)
@@ -106,10 +109,10 @@
     new_numerator, new_weight, debiased = call(
         mix_kernel,
         (shard, jax.ShapeDtypeStruct((1,), jnp.float32), jax.ShapeDtypeStruct(half.shape, jnp.bfloat16)),
-        [scalars] + [arrays] * 2,
+        [arrays] * 3,
         (arrays, scalars, arrays),
         8 * half.size,
-    )(weight, half, partner)
+    )(half, payload, partner)
     return (new_numerator[None], new_weight, debiased[None], new_moment1[None], new_moment2[None])
 
 
@@ -134,7 +137,7 @@
     )(first_corr, second_corr, weight, landed, numerator[0], moment1[0], moment2[0])
     branches = [partial(exchanged, offset=1 << level) for level in range(levels)]
     return lax.switch(
-        step[0] % levels, branches, weight, landed, moment1[0], moment2[0], half, payload
+        step[0] % levels, branches, landed, moment1[0], moment2[0], half, payload
     )
 
 

time: 46.7 us -> 37.9 us (0.81)
  the two profiles are of different devices: /device:TPU:102 before, /device:TPU:4 now
where the time goes in v3:
time: 37.9 us; the launch traced here: 37.7 us
  waiting for transfers between devices  22 us (58%)
  starting transfers between devices  11.4 us (30%)
  Pallas kernels  2.16 us (6%)
  between operations  2.06 us (5%)
    ppermute x1, waiting for transfers between devices, shifted(): return lax.ppermute(value, axis, pairs)  11.1 us
    all_to_all x1, waiting for transfers between devices, local(): lax.all_to_all(blocks, 'fsdp', split_axis=0, concat_axis=0, tiled=True)  10.9 us
    all_to_all x1, starting transfers between devices, local(): lax.all_to_all(blocks, 'fsdp', split_axis=0, concat_axis=0, tiled=True)  9.5 us
    ppermute x1, starting transfers between devices, shifted(): return lax.ppermute(value, axis, pairs)  1.92 us
    pallas_call x1, Pallas kernels, exchanged(): call(moments_kernel, (shard, shard), [arrays] * 3, (arrays,) * 2, 4 * lan...  0.99 us
    pallas_call x1, Pallas kernels, exchanged(): call(mix_kernel, (shard, jax.ShapeDtypeStruct((1,), jnp.float32), jax.Sha...  0.81 us
  transfers between devices with their start and end apart: 2, of which 2 were waited for; matrix products, arithmetic and copies ran while one was open for 0% of the time, Pallas kernels for 3%

profile of v3, /device:TPU:4, one launch (start us, length us, event | category | flops | bytes accessed | tf_op | source)
XLA Modules:
  0.0 37.7 jit_solution(10306852021647115558)
XLA Ops:
  0.6 0.0 copy-start
  0.6 0.0 copy-start.1
  0.7 0.0 copy-start.2
  0.7 9.5 %all-to-all-start = ((bf16[8,64,1024]{2,1,0:T(8,128)(2,1)}), bf16[8,64,1024]{2,1,0:T(8,128)(2,1)S(1)}, u32[]{:S(2)}, u32[]{:S(2)}) async-start(bf16[8,64,1024]{2,1,0:T(8,128)(2,1)} %bitcast.44), calls=%async_computation | async-start | bytes 2097152 | tf_op jit(solution)/shard_map/all_to_all | solution.py:127
  11.6 10.9 %all-to-all-done.landed_ref = bf16[8,64,1024]{2,1,0:T(8,128)(2,1)S(1)} async-done(((bf16[8,64,1024]{2,1,0:T(8,128)(2,1)}), bf16[8,64,1024]{2,1,0:T(8,128)(2,1)S(1)}, u32[]{:S(2)}, u32[]{:S(2)}) %all-to-all-start) | async-done | bytes 1048608 | tf_op jit(solution)/shard_map/all_to_all | solution.py:127
  22.5 0.0 copy-done
  22.5 0.0 copy-done.1
  22.5 0.0 copy-done.2
  22.5 0.4 adam_kernel.1
  22.9 14.8 %conditional.1 = (f32[1]{0:T(128)}, f32[1,64,1024]{2,1,0:T(8,128)}, bf16[1,64,1024]{2,1,0:T(8,128)(2,1)}, f32[1,64,1024]{2,1,0:T(8,128)}, f32[1,64,1024]{2,1,0:T(8,128)}) conditional(s32[]{:T(128)} %clamp.3, (bf16[528,128]{1,0:T(8,128)(2,1)S(1)}, f32[64,1024]{1,0:T(8,128)S(1)}, bf16[8,64,1024]{2,1,0:T(8,128)(2,1)S(1)}, ...), branch_computations={%region_0.1_spmd, %region_1.2_spmd, %region_2.3_spmd, %region_3.4_... | conditional | flops 2621440 | bytes 3162192 | solution.py:139
  22.9 1.9 %collective-permute-start = (bf16[528,128]{1,0:T(8,128)(2,1)S(1)}, bf16[528,128]{1,0:T(8,128)(2,1)S(1)}, u32[]{:S(2)}, u32[]{:S(2)}) collective-permute-start(bf16[528,128]{1,0:T(8,128)(2,1)S(1)} %get-tuple-element.61.own_ref), channel_id=1, source_target_pairs={{0,8},{8,16},{16,24},{24,32},{32,40},{40,48},{48,56},{56,64},{64,7... | collective-permute-start | bytes 405512 | tf_op jit(solution)/shard_map/cond/branch_0_fun/ppermute | solution.py:17
  24.8 1.0 %moments_kernel.6 = (f32[64,1024]{1,0:T(8,128)}, f32[64,1024]{1,0:T(8,128)}) custom-call(bf16[8,64,1024]{2,1,0:T(8,128)(2,1)S(1)} %get-tuple-element.65.landed_ref, f32[64,1024]{1,0:T(8,128)S(1)} %get-tuple-element.66.moment1_ref, f32[64,1024]{1,0:T(8,128)S(1)} %get-tuple-element.67.moment2_ref), custom_call_target="tpu_custom_call" | custom-call | flops 2097152 | bytes 2097152 | tf_op jit(solution)/shard_map/cond/branch_0_fun/moments_kernel/pallas_call | solution.py:106
  25.8 11.1 %collective-permute-done.partner_ref = bf16[528,128]{1,0:T(8,128)(2,1)S(1)} collective-permute-done((bf16[528,128]{1,0:T(8,128)(2,1)S(1)}, bf16[528,128]{1,0:T(8,128)(2,1)S(1)}, u32[]{:S(2)}, u32[]{:S(2)}) %collective-permute-start) | collective-permute-done | bytes 135200 | tf_op jit(solution)/shard_map/cond/branch_0_fun/ppermute | solution.py:17
  36.9 0.8 %mix_kernel.6 = (f32[64,1024]{1,0:T(8,128)}, f32[1]{0:T(128)}, bf16[64,1024]{1,0:T(8,128)(2,1)}) custom-call(f32[64,1024]{1,0:T(8,128)S(1)} %get-tuple-element.60.half_ref, bf16[528,128]{1,0:T(8,128)(2,1)S(1)} %get-tuple-element.61.own_ref, bf16[528,128]{1,0:T(8,128)(2,1)S(1)} %collective-permute-done.partner_ref), custom_call_target="tpu_custom_call" | custom-call | flops 524288 | bytes 524288 | tf_op jit(solution)/shard_map/cond/branch_0_fun/mix_kernel/pallas_call | solution.py:109
Async XLA Ops:
  0.6 21.9 %copy-start = (f32[1,64,1024]{2,1,0:T(8,128)S(1)}, f32[1,64,1024]{2,1,0:T(8,128)}, u32[]{:S(2)}) copy-start(f32[1,64,1024]{2,1,0:T(8,128)} %param.13) | copy-start | bytes 786436
  0.6 21.8 %copy-start.1 = (f32[1,64,1024]{2,1,0:T(8,128)S(1)}, f32[1,64,1024]{2,1,0:T(8,128)}, u32[]{:S(2)}) copy-start(f32[1,64,1024]{2,1,0:T(8,128)} %param.15) | copy-start | bytes 786436
  0.7 21.8 %copy-start.2 = (f32[1,64,1024]{2,1,0:T(8,128)S(1)}, f32[1,64,1024]{2,1,0:T(8,128)}, u32[]{:S(2)}) copy-start(f32[1,64,1024]{2,1,0:T(8,128)} %param.16) | copy-start | bytes 786436
  0.7 21.8 %all-to-all-start = ((bf16[8,64,1024]{2,1,0:T(8,128)(2,1)}), bf16[8,64,1024]{2,1,0:T(8,128)(2,1)S(1)}, u32[]{:S(2)}, u32[]{:S(2)}) async-start(bf16[8,64,1024]{2,1,0:T(8,128)(2,1)} %bitcast.44), calls=%async_computation | async-start | bytes 2097152 | tf_op jit(solution)/shard_map/all_to_all | solution.py:127
  22.9 14.0 %collective-permute-start = (bf16[528,128]{1,0:T(8,128)(2,1)S(1)}, bf16[528,128]{1,0:T(8,128)(2,1)S(1)}, u32[]{:S(2)}, u32[]{:S(2)}) collective-permute-start(bf16[528,128]{1,0:T(8,128)(2,1)S(1)} %get-tuple-element.61.own_ref), channel_id=1, source_target_pairs={{0,8},{8,16},{16,24},{24,32},{32,40},{40,48},{48,56},{56,64},{64,7... | collective-permute-start | bytes 405512 | tf_op jit(solution)/shard_map/cond/branch_0_fun/ppermute | solution.py:17

commit v4 on v3

--- a/solution.py
+++ b/solution.py
@@ -13,8 +13,11 @@
 
 def shifted(value, axis, steps):
     count = lax.axis_size(axis)
-    pairs = [(source, (source + steps) % count) for source in range(count)]
-    return lax.ppermute(value, axis, pairs)
+    around = [(source, source + steps - count) for source in range(count - steps, count)]
+    onward = [(source, source + steps) for source in range(count - steps)]
+    if 2 * steps == count:
+        return (lax.ppermute(value, axis, around + onward),)
+    return lax.ppermute(value, axis, onward), lax.ppermute(value, axis, around)
 
 
 def tiles_of(shape):
@@ -67,18 +70,22 @@
     payload_ref[pl.ds(payload_ref.shape[0] - TILE_ROWS, TILE_ROWS), :] = terms.astype(jnp.bfloat16)
 
 
-def weight_in(payload_ref):
-    tail = pl.ds(payload_ref.shape[0] - TILE_ROWS, TILE_ROWS)
-    terms = payload_ref[tail, :].astype(jnp.float32)
+def received(rows, *refs):
+    return sum(ref[rows, :].astype(jnp.float32) for ref in refs)
+
+
+def weight_in(*refs):
+    terms = received(pl.ds(refs[0].shape[0] - TILE_ROWS, TILE_ROWS), *refs)
     return terms[0:1] + (terms[1:2] + terms[2:3])
 
 
-def mix_kernel(half_ref, own_ref, partner_ref, new_numerator_ref, new_weight_ref, debiased_ref):
-    new_weight = 0.5 * (weight_in(own_ref) + weight_in(partner_ref))
+def mix_kernel(half_ref, own_ref, *refs):
+    sent_refs, (new_numerator_ref, new_weight_ref, debiased_ref) = refs[:-3], refs[-3:]
+    new_weight = 0.5 * (weight_in(own_ref) + weight_in(*sent_refs))
     new_weight_ref[0] = new_weight[0, 0]
     scale = 1.0 / new_weight
     for rows, lanes, packed in tiles_of(half_ref.shape):
-        mixed = 0.5 * (half_ref[rows, lanes] + partner_ref[packed, :].astype(jnp.float32))
+        mixed = 0.5 * (half_ref[rows, lanes] + received(packed, *sent_refs))
         new_numerator_ref[rows, lanes] = mixed
         debiased_ref[rows, lanes] = (mixed * scale).astype(jnp.bfloat16)
 
@@ -102,17 +109,17 @@
 def exchanged(landed, moment1, moment2, half, payload, offset):
     shard = jax.ShapeDtypeStruct(half.shape, jnp.float32)
     scalars, arrays = spec(pltpu.SMEM), spec(pltpu.VMEM)
-    partner = shifted(payload, "rep", offset)
+    sent = shifted(payload, "rep", offset)
     new_moment1, new_moment2 = call(
         moments_kernel, (shard, shard), [arrays] * 3, (arrays,) * 2, 4 * landed.size
     )(landed, moment1, moment2)
     new_numerator, new_weight, debiased = call(
         mix_kernel,
         (shard, jax.ShapeDtypeStruct((1,), jnp.float32), jax.ShapeDtypeStruct(half.shape, jnp.bfloat16)),
-        [arrays] * 3,
+        [arrays] * (2 + len(sent)),
         (arrays, scalars, arrays),
         8 * half.size,
-    )(half, payload, partner)
+    )(half, payload, *sent)
     return (new_numerator[None], new_weight, debiased[None], new_moment1[None], new_moment2[None])
 
 

time: 37.9 us -> 45.5 us (1.20)
  the two profiles are of different devices: /device:TPU:4 before, /device:TPU:102 now
where the time goes in v4:
time: 45.5 us; the launch traced here: 45.2 us
  waiting for transfers between devices  23.6 us (52%)
  starting transfers between devices  17.3 us (38%)
  Pallas kernels  2.18 us (5%)
  between operations  2.06 us (5%)
    all_to_all x1, waiting for transfers between devices, local(): lax.all_to_all(blocks, 'fsdp', split_axis=0, concat_axis=0, tiled=True)  12.8 us
    ppermute x1, waiting for transfers between devices, shifted(): lax.ppermute(value, axis, around)  10.7 us
    ppermute x1, starting transfers between devices, shifted(): lax.ppermute(value, axis, onward)  8.48 us
    all_to_all x1, starting transfers between devices, local(): lax.all_to_all(blocks, 'fsdp', split_axis=0, concat_axis=0, tiled=True)  7.58 us
    ppermute x1, starting transfers between devices, shifted(): lax.ppermute(value, axis, around)  1.29 us
    pallas_call x1, Pallas kernels, exchanged(): call(moments_kernel, (shard, shard), [arrays] * 3, (arrays,) * 2, 4 * lan...  0.99 us
  transfers between devices with their start and end apart: 3, of which 2 were waited for; matrix products, arithmetic and copies ran while one was open for 0% of the time, Pallas kernels for 2%

profile of v4, /device:TPU:102, one launch (start us, length us, event | category | flops | bytes accessed | tf_op | source)
XLA Modules:
  0.0 45.2 jit_solution(898524303752127501)
XLA Ops:
  0.6 0.0 copy-start
  0.6 0.0 copy-start.1
  0.7 0.0 copy-start.2
  0.7 7.6 %all-to-all-start = ((bf16[8,64,1024]{2,1,0:T(8,128)(2,1)}), bf16[8,64,1024]{2,1,0:T(8,128)(2,1)S(1)}, u32[]{:S(2)}, u32[]{:S(2)}) async-start(bf16[8,64,1024]{2,1,0:T(8,128)(2,1)} %bitcast.44), calls=%async_computation | async-start | bytes 2097152 | tf_op jit(solution)/shard_map/all_to_all | solution.py:134
  9.6 12.8 %all-to-all-done.landed_ref = bf16[8,64,1024]{2,1,0:T(8,128)(2,1)S(1)} async-done(((bf16[8,64,1024]{2,1,0:T(8,128)(2,1)}), bf16[8,64,1024]{2,1,0:T(8,128)(2,1)S(1)}, u32[]{:S(2)}, u32[]{:S(2)}) %all-to-all-start) | async-done | bytes 1048608 | tf_op jit(solution)/shard_map/all_to_all | solution.py:134
  22.5 0.0 copy-done
  22.5 0.0 copy-done.1
  22.5 0.0 copy-done.2
  22.5 0.4 adam_kernel.1
  22.9 22.4 %conditional.1 = (f32[1]{0:T(128)}, f32[1,64,1024]{2,1,0:T(8,128)}, bf16[1,64,1024]{2,1,0:T(8,128)(2,1)}, f32[1,64,1024]{2,1,0:T(8,128)}, f32[1,64,1024]{2,1,0:T(8,128)}) conditional(s32[]{:T(128)} %clamp.3, (bf16[528,128]{1,0:T(8,128)(2,1)S(1)}, f32[64,1024]{1,0:T(8,128)S(1)}, bf16[8,64,1024]{2,1,0:T(8,128)(2,1)S(1)}, ...), branch_computations={%region_0.1_spmd, %region_1.2_spmd, %region_2.3_spmd, %region_3.4_... | conditional | flops 2621440 | bytes 3702904 | solution.py:146
  22.9 1.3 %collective-permute-start.9 = (bf16[528,128]{1,0:T(8,128)(2,1)S(1)}, bf16[528,128]{1,0:T(8,128)(2,1)S(1)}, u32[]{:S(2)}, u32[]{:S(2)}) collective-permute-start(bf16[528,128]{1,0:T(8,128)(2,1)S(1)} %get-tuple-element.101.own_ref), channel_id=1, source_target_pairs={{384,0},{392,8},{400,16},{408,24},{416,32},{424,40},{432,48},{440,... | collective-permute-start | bytes 405512 | tf_op jit(solution)/shard_map/cond/branch_4_fun/ppermute | solution.py:20
  24.2 8.5 %collective-permute-start.8 = (bf16[528,128]{1,0:T(8,128)(2,1)S(1)}, bf16[528,128]{1,0:T(8,128)(2,1)S(1)}, u32[]{:S(2)}, u32[]{:S(2)}) collective-permute-start(bf16[528,128]{1,0:T(8,128)(2,1)S(1)} %get-tuple-element.101.own_ref), channel_id=1, source_target_pairs={{0,128},{8,136},{16,144},{24,152},{32,160},{40,168},{48,176},{56,1... | collective-permute-start | bytes 405512 | tf_op jit(solution)/shard_map/cond/branch_4_fun/ppermute | solution.py:20
  32.7 1.0 %moments_kernel.10 = (f32[64,1024]{1,0:T(8,128)}, f32[64,1024]{1,0:T(8,128)}) custom-call(bf16[8,64,1024]{2,1,0:T(8,128)(2,1)S(1)} %get-tuple-element.105.landed_ref, f32[64,1024]{1,0:T(8,128)S(1)} %get-tuple-element.106.moment1_ref, f32[64,1024]{1,0:T(8,128)S(1)} %get-tuple-element.107.moment2_ref), custom_call_target="tpu_custom_call" | custom-call | flops 2097152 | bytes 2097152 | tf_op jit(solution)/shard_map/cond/branch_4_fun/moments_kernel/pallas_call | solution.py:113
  33.7 10.7 %collective-permute-done.9.refs_1_ = bf16[528,128]{1,0:T(8,128)(2,1)S(1)} collective-permute-done((bf16[528,128]{1,0:T(8,128)(2,1)S(1)}, bf16[528,128]{1,0:T(8,128)(2,1)S(1)}, u32[]{:S(2)}, u32[]{:S(2)}) %collective-permute-start.9) | collective-permute-done | bytes 135200 | tf_op jit(solution)/shard_map/cond/branch_4_fun/ppermute | solution.py:20
  44.4 0.0 collective-permute-done.8.refs_0_
  44.4 0.8 %mix_kernel.10 = (f32[64,1024]{1,0:T(8,128)}, f32[1]{0:T(128)}, bf16[64,1024]{1,0:T(8,128)(2,1)}) custom-call(f32[64,1024]{1,0:T(8,128)S(1)} %get-tuple-element.100.half_ref, bf16[528,128]{1,0:T(8,128)(2,1)S(1)} %get-tuple-element.101.own_ref, bf16[528,128]{1,0:T(8,128)(2,1)S(1)} %collective-permute-done.8.refs_0_, ...), custom_call_target="tpu_custom_call" | custom-call | flops 524288 | bytes 524288 | tf_op jit(solution)/shard_map/cond/branch_4_fun/mix_kernel/pallas_call | solution.py:116
Async XLA Ops:
  0.6 21.9 %copy-start = (f32[1,64,1024]{2,1,0:T(8,128)S(1)}, f32[1,64,1024]{2,1,0:T(8,128)}, u32[]{:S(2)}) copy-start(f32[1,64,1024]{2,1,0:T(8,128)} %param.13) | copy-start | bytes 786436
  0.6 21.8 %copy-start.1 = (f32[1,64,1024]{2,1,0:T(8,128)S(1)}, f32[1,64,1024]{2,1,0:T(8,128)}, u32[]{:S(2)}) copy-start(f32[1,64,1024]{2,1,0:T(8,128)} %param.15) | copy-start | bytes 786436
  0.7 21.8 %copy-start.2 = (f32[1,64,1024]{2,1,0:T(8,128)S(1)}, f32[1,64,1024]{2,1,0:T(8,128)}, u32[]{:S(2)}) copy-start(f32[1,64,1024]{2,1,0:T(8,128)} %param.16) | copy-start | bytes 786436
  0.7 21.8 %all-to-all-start = ((bf16[8,64,1024]{2,1,0:T(8,128)(2,1)}), bf16[8,64,1024]{2,1,0:T(8,128)(2,1)S(1)}, u32[]{:S(2)}, u32[]{:S(2)}) async-start(bf16[8,64,1024]{2,1,0:T(8,128)(2,1)} %bitcast.44), calls=%async_computation | async-start | bytes 2097152 | tf_op jit(solution)/shard_map/all_to_all | solution.py:134
  22.9 21.5 %collective-permute-start.9 = (bf16[528,128]{1,0:T(8,128)(2,1)S(1)}, bf16[528,128]{1,0:T(8,128)(2,1)S(1)}, u32[]{:S(2)}, u32[]{:S(2)}) collective-permute-start(bf16[528,128]{1,0:T(8,128)(2,1)S(1)} %get-tuple-element.101.own_ref), channel_id=1, source_target_pairs={{384,0},{392,8},{400,16},{408,24},{416,32},{424,40},{432,48},{440,... | collective-permute-start | bytes 405512 | tf_op jit(solution)/shard_map/cond/branch_4_fun/ppermute | solution.py:20
  24.2 20.2 %collective-permute-start.8 = (bf16[528,128]{1,0:T(8,128)(2,1)S(1)}, bf16[528,128]{1,0:T(8,128)(2,1)S(1)}, u32[]{:S(2)}, u32[]{:S(2)}) collective-permute-start(bf16[528,128]{1,0:T(8,128)(2,1)S(1)} %get-tuple-element.101.own_ref), channel_id=1, source_target_pairs={{0,128},{8,136},{16,144},{24,152},{32,160},{40,168},{48,176},{56,1... | collective-permute-start | bytes 405512 | tf_op jit(solution)/shard_map/cond/branch_4_fun/ppermute | solution.py:20

commit v5 on v4

--- a/solution.py
+++ b/solution.py
@@ -15,9 +15,11 @@
     count = lax.axis_size(axis)
     around = [(source, source + steps - count) for source in range(count - steps, count)]
     onward = [(source, source + steps) for source in range(count - steps)]
+    first, second = around, onward
     if 2 * steps == count:
-        return (lax.ppermute(value, axis, around + onward),)
-    return lax.ppermute(value, axis, onward), lax.ppermute(value, axis, around)
+        first = [pair for pair in around + onward if pair[0] % 2 == 1]
+        second = [pair for pair in around + onward if pair[0] % 2 == 0]
+    return lax.ppermute(value, axis, second), lax.ppermute(value, axis, first)
 
 
 def tiles_of(shape):

time: 45.5 us -> 50.6 us (1.11)
  the two profiles are of different devices: /device:TPU:102 before, /device:TPU:38 now
where the time goes in v5:
time: 50.6 us; the launch traced here: 50.4 us
  starting transfers between devices  23.1 us (46%)
  waiting for transfers between devices  23 us (45%)
  Pallas kernels  2.18 us (4%)
  between operations  2.06 us (4%)
    ppermute x2, starting transfers between devices, shifted(): return (lax.ppermute(value, axis, second), lax.ppermute(value, axis, first))  15.5 us
    all_to_all x1, waiting for transfers between devices, local(): lax.all_to_all(blocks, 'fsdp', split_axis=0, concat_axis=0, tiled=True)  12.8 us
    ppermute x2, waiting for transfers between devices, shifted(): return (lax.ppermute(value, axis, second), lax.ppermute(value, axis, first))  10.2 us
    all_to_all x1, starting transfers between devices, local(): lax.all_to_all(blocks, 'fsdp', split_axis=0, concat_axis=0, tiled=True)  7.58 us
  transfers between devices with their start and end apart: 3, of which 2 were waited for; matrix products, arithmetic and copies ran while one was open for 0% of the time, Pallas kernels for 2%

profile of v5, /device:TPU:38, one launch (start us, length us, event | category | flops | bytes accessed | tf_op | source)
XLA Modules:
  0.0 50.4 jit_solution(10625294576194689098)
XLA Ops:
  0.6 0.0 copy-start
  0.6 0.0 copy-start.1
  0.7 0.0 copy-start.2
  0.7 7.6 %all-to-all-start = ((bf16[8,64,1024]{2,1,0:T(8,128)(2,1)}), bf16[8,64,1024]{2,1,0:T(8,128)(2,1)S(1)}, u32[]{:S(2)}, u32[]{:S(2)}) async-start(bf16[8,64,1024]{2,1,0:T(8,128)(2,1)} %bitcast.44), calls=%async_computation | async-start | bytes 2097152 | tf_op jit(solution)/shard_map/all_to_all | solution.py:136
  9.6 12.8 %all-to-all-done.landed_ref = bf16[8,64,1024]{2,1,0:T(8,128)(2,1)S(1)} async-done(((bf16[8,64,1024]{2,1,0:T(8,128)(2,1)}), bf16[8,64,1024]{2,1,0:T(8,128)(2,1)S(1)}, u32[]{:S(2)}, u32[]{:S(2)}) %all-to-all-start) | async-done | bytes 1048608 | tf_op jit(solution)/shard_map/all_to_all | solution.py:136
  22.5 0.0 copy-done
  22.5 0.0 copy-done.1
  22.5 0.0 copy-done.2
  22.5 0.4 adam_kernel.1
  22.9 27.5 %conditional.1 = (f32[1]{0:T(128)}, f32[1,64,1024]{2,1,0:T(8,128)}, bf16[1,64,1024]{2,1,0:T(8,128)(2,1)}, f32[1,64,1024]{2,1,0:T(8,128)}, f32[1,64,1024]{2,1,0:T(8,128)}) conditional(s32[]{:T(128)} %clamp.3, (bf16[528,128]{1,0:T(8,128)(2,1)S(1)}, f32[64,1024]{1,0:T(8,128)S(1)}, bf16[8,64,1024]{2,1,0:T(8,128)(2,1)S(1)}, ...), branch_computations={%region_0.1_spmd, %region_1.2_spmd, %region_2.3_spmd, %region_3.4_... | conditional | flops 2621440 | bytes 3702904 | solution.py:148
  22.9 0.7 %collective-permute-start.11 = (bf16[528,128]{1,0:T(8,128)(2,1)S(1)}, bf16[528,128]{1,0:T(8,128)(2,1)S(1)}, u32[]{:S(2)}, u32[]{:S(2)}) collective-permute-start(bf16[528,128]{1,0:T(8,128)(2,1)S(1)} %get-tuple-element.111.own_ref), channel_id=1, source_target_pairs={{264,8},{280,24},{296,40},{312,56},{328,72},{344,88},{360,104},{37... | collective-permute-start | bytes 405512 | tf_op jit(solution)/shard_map/cond/branch_5_fun/ppermute | solution.py:22
  23.6 14.8 %collective-permute-start.10 = (bf16[528,128]{1,0:T(8,128)(2,1)S(1)}, bf16[528,128]{1,0:T(8,128)(2,1)S(1)}, u32[]{:S(2)}, u32[]{:S(2)}) collective-permute-start(bf16[528,128]{1,0:T(8,128)(2,1)S(1)} %get-tuple-element.111.own_ref), channel_id=1, source_target_pairs={{256,0},{272,16},{288,32},{304,48},{320,64},{336,80},{352,96},{368... | collective-permute-start | bytes 405512 | tf_op jit(solution)/shard_map/cond/branch_5_fun/ppermute | solution.py:22
  38.4 1.0 %moments_kernel.11 = (f32[64,1024]{1,0:T(8,128)}, f32[64,1024]{1,0:T(8,128)}) custom-call(bf16[8,64,1024]{2,1,0:T(8,128)(2,1)S(1)} %get-tuple-element.115.landed_ref, f32[64,1024]{1,0:T(8,128)S(1)} %get-tuple-element.116.moment1_ref, f32[64,1024]{1,0:T(8,128)S(1)} %get-tuple-element.117.moment2_ref), custom_call_target="tpu_custom_call" | custom-call | flops 2097152 | bytes 2097152 | tf_op jit(solution)/shard_map/cond/branch_5_fun/moments_kernel/pallas_call | solution.py:115
  39.4 0.0 collective-permute-done.11.refs_1_
  39.4 10.2 %collective-permute-done.10.refs_0_ = bf16[528,128]{1,0:T(8,128)(2,1)S(1)} collective-permute-done((bf16[528,128]{1,0:T(8,128)(2,1)S(1)}, bf16[528,128]{1,0:T(8,128)(2,1)S(1)}, u32[]{:S(2)}, u32[]{:S(2)}) %collective-permute-start.10) | collective-permute-done | bytes 135200 | tf_op jit(solution)/shard_map/cond/branch_5_fun/ppermute | solution.py:22
  49.6 0.8 %mix_kernel.11 = (f32[64,1024]{1,0:T(8,128)}, f32[1]{0:T(128)}, bf16[64,1024]{1,0:T(8,128)(2,1)}) custom-call(f32[64,1024]{1,0:T(8,128)S(1)} %get-tuple-element.110.half_ref, bf16[528,128]{1,0:T(8,128)(2,1)S(1)} %get-tuple-element.111.own_ref, bf16[528,128]{1,0:T(8,128)(2,1)S(1)} %collective-permute-done.10.refs_0_, ...), custom_call_target="tpu_custom_call" | custom-call | flops 524288 | bytes 524288 | tf_op jit(solution)/shard_map/cond/branch_5_fun/mix_kernel/pallas_call | solution.py:118
Async XLA Ops:
  0.6 21.9 %copy-start = (f32[1,64,1024]{2,1,0:T(8,128)S(1)}, f32[1,64,1024]{2,1,0:T(8,128)}, u32[]{:S(2)}) copy-start(f32[1,64,1024]{2,1,0:T(8,128)} %param.13) | copy-start | bytes 786436
  0.6 21.8 %copy-start.1 = (f32[1,64,1024]{2,1,0:T(8,128)S(1)}, f32[1,64,1024]{2,1,0:T(8,128)}, u32[]{:S(2)}) copy-start(f32[1,64,1024]{2,1,0:T(8,128)} %param.15) | copy-start | bytes 786436
  0.7 21.8 %copy-start.2 = (f32[1,64,1024]{2,1,0:T(8,128)S(1)}, f32[1,64,1024]{2,1,0:T(8,128)}, u32[]{:S(2)}) copy-start(f32[1,64,1024]{2,1,0:T(8,128)} %param.16) | copy-start | bytes 786436
  0.7 21.8 %all-to-all-start = ((bf16[8,64,1024]{2,1,0:T(8,128)(2,1)}), bf16[8,64,1024]{2,1,0:T(8,128)(2,1)S(1)}, u32[]{:S(2)}, u32[]{:S(2)}) async-start(bf16[8,64,1024]{2,1,0:T(8,128)(2,1)} %bitcast.44), calls=%async_computation | async-start | bytes 2097152 | tf_op jit(solution)/shard_map/all_to_all | solution.py:136
  22.9 16.5 %collective-permute-start.11 = (bf16[528,128]{1,0:T(8,128)(2,1)S(1)}, bf16[528,128]{1,0:T(8,128)(2,1)S(1)}, u32[]{:S(2)}, u32[]{:S(2)}) collective-permute-start(bf16[528,128]{1,0:T(8,128)(2,1)S(1)} %get-tuple-element.111.own_ref), channel_id=1, source_target_pairs={{264,8},{280,24},{296,40},{312,56},{328,72},{344,88},{360,104},{37... | collective-permute-start | bytes 405512 | tf_op jit(solution)/shard_map/cond/branch_5_fun/ppermute | solution.py:22
  23.6 26.0 %collective-permute-start.10 = (bf16[528,128]{1,0:T(8,128)(2,1)S(1)}, bf16[528,128]{1,0:T(8,128)(2,1)S(1)}, u32[]{:S(2)}, u32[]{:S(2)}) collective-permute-start(bf16[528,128]{1,0:T(8,128)(2,1)S(1)} %get-tuple-element.111.own_ref), channel_id=1, source_target_pairs={{256,0},{272,16},{288,32},{304,48},{320,64},{336,80},{352,96},{368... | collective-permute-start | bytes 405512 | tf_op jit(solution)/shard_map/cond/branch_5_fun/ppermute | solution.py:22
